TPU v7x, 512 devices: a whole 4x8x8 slice. The times are simulated.
512 devices in a mesh: pair: 32 (over y, z_lo), virt: 16 (over x, z_hi, core).
Axes of the slice: x: 4, y: 8, z: 8 (z_hi: 2, z_lo: 4; z = z_hi * 4 + z_lo), core: 2. Of those that a mesh axis runs over, the one named last changes fastest.
Arguments:
- amplitudes: bfloat16 [16384, 6144], P('pair', 'virt'), may hold values from -6 to 6
- integrals: bfloat16 [6144, 6144], P('pair', 'virt'), may hold values from -0.21875 to 0.21875
- irreps: int32 [768], replicated, may hold values from 0 to 7, as said below
Outputs:
- ladder: bfloat16 [16384, 6144], P('pair', 'virt')
Inputs may be any that keep to these rules, and one draw needn't show every extreme that they name: irreps never falls along the orbitals; each irrep 0 to 7 occupies one block of one or more whole tiles of 64 orbitals, and every irrep appears.
All inputs are finite; a program needn't handle non-finite values.
Results may differ from a plain program's by a relative error of at most 0.001.
Values may be sent and summed in bfloat16 or wider, within the bound.
A program may use at most 64 MiB of HBM per device.

v0:
```python
import jax
import jax.numpy as jnp
from jax import lax
from jax.sharding import PartitionSpec as P


def per_device(amplitudes, integrals, irreps):
    nvir = irreps.shape[0]
    virt_count = lax.axis_size("virt")
    local_cols = integrals.shape[1]
    krows_all = amplitudes.shape[1] * virt_count
    slab_c = krows_all // nvir
    slab_a = local_cols * virt_count // nvir
    row_sym = jnp.bitwise_xor(irreps[:slab_c, None], irreps[None, :]).reshape(-1)
    col_sym_all = jnp.bitwise_xor(irreps[:slab_a, None], irreps[None, :]).reshape(-1)
    col_first = lax.axis_index("virt") * local_cols
    col_sym = lax.dynamic_slice_in_dim(col_sym_all, col_first, local_cols, 0)
    gathered = lax.all_gather(amplitudes, "virt", axis=1, tiled=True)
    slab_part = lax.all_gather(integrals, "pair", axis=0, tiled=True)
    masked = jnp.where(row_sym[:, None] == col_sym[None, :], slab_part, jnp.zeros_like(slab_part))
    ladder = jnp.dot(gathered, masked, preferred_element_type=jnp.float32)
    return ladder.astype(jnp.bfloat16)


def solution(mesh):
    placed = (P("pair", "virt"), P("pair", "virt"), P())
    return jax.shard_map(
        per_device, mesh=mesh, in_specs=placed, out_specs=P("pair", "virt"), check_vma=False
    )
```

profile of v0, /device:TPU:1, one launch (start us, length us, event | category | flops | bytes accessed | tf_op | source)
XLA Modules:
  0.0 297.3 jit_solution(14039116942693812781)
XLA Ops:
  6.5 0.0 all-gather.3.cloned.1.call-start
  6.5 0.7 all-gather.3.cloned.1.call-update
  7.3 0.0 all-gather.5.cloned.1.call-start
  7.3 0.7 all-gather.5.cloned.1.call-update
  8.0 0.7 slice.4
  8.7 0.8 broadcast_xor_fusion
  9.5 0.1 dynamic_slice.3
  9.5 146.7 %all-gather.3.cloned.1.call-done = bf16[6144,384]{1,0:T(8,128)(2,1)} async-done(((bf16[192,384]{1,0:T(8,128)(2,1)}), bf16[6144,384]{1,0:T(8,128)(2,1)}) %all-gather.3.cloned.1.call-update) | async-done | bytes 4718608 | tf_op jit(solution)/shard_map/all_gather | solution.py:19
  156.2 126.4 %all-gather.5.cloned.1.call-done = bf16[512,6144]{1,0:T(8,128)(2,1)} async-done(((bf16[512,384]{1,0:T(8,128)(2,1)}), bf16[512,6144]{1,0:T(8,128)(2,1)}) %all-gather.5.cloned.1.call-update) | async-done | bytes 6291472 | tf_op jit(solution)/shard_map/all_gather | solution.py:18
  282.6 7.0 %fusion.5 = bf16[512,384]{0,1:T(8,128)(2,1)S(1)} fusion(bf16[512,6144]{1,0:T(8,128)(2,1)} %all-gather.5.cloned.1.call-done, bf16[6144,384]{1,0:T(8,128)(2,1)} %all-gather.3.cloned.1.call-done, s32[384]{0:T(512)S(1)} %dynamic_slice.3, s32[6144]{0:T(1024)S(1)} %xor.31), kind=kOutput, calls=%fused_computation.6 | convolution fusion | flops 2420834304 | bytes 11429376 | tf_op jit(solution)/shard_map/dot_general | solution.py:21
  289.5 0.9 copy.4
  (1 shorter events, 0.0 us)
Async XLA Ops:
  6.5 149.7 %all-gather.3.cloned.1.call-start = ((), (), s32[]{:S(2)}) async-start(), calls=%async_computation | async-start | bytes 4866048 | tf_op jit(solution)/shard_map/all_gather | solution.py:19
  7.3 275.3 %all-gather.5.cloned.1.call-start = ((), (), s32[]{:S(2)}) async-start(), calls=%async_computation.1 | async-start | bytes 6684672 | tf_op jit(solution)/shard_map/all_gather | solution.py:18
Sparse Core Ops, SparseCore 0:
  9.4 146.7 all-gather.2
  159.3 123.1 all-gather.4
where the time goes:
time: 297 us
  waiting for transfers between devices  274 us (92%)
  between operations  13.4 us (5%)
  matrix products  6.99 us (2%)
    all_gather x1, waiting for transfers between devices, per_device(): slab_part = lax.all_gather(integrals, 'pair', axis=0, tiled=True)  147 us
    all_gather x1, waiting for transfers between devices, per_device(): gathered = lax.all_gather(amplitudes, 'virt', axis=1, tiled=True)  126 us
    dot_general x1, matrix products, per_device(): ladder = jnp.dot(gathered, masked, preferred_element_type=jnp.float32)  6.99 us
  transfers between devices with their start and end apart: 2, of which 2 were waited for; matrix products, arithmetic and copies ran while one was open for 1% of the time, Pallas kernels for 0%

commit v1 on v0

v1 whole, which is shorter than its diff:
```python
import jax
import jax.numpy as jnp
from jax import lax
from jax.experimental import pallas as pl
from jax.experimental.pallas import tpu as pltpu
from jax.sharding import PartitionSpec as P

MESH = pl.DeviceIdType.MESH
BF16 = jnp.bfloat16
F32 = jnp.float32
TILE = 64
TILES = 12
BINS = 4
BIN = 192
NVIR = 768
HALF = 384
CHUNKS = 4
RC = 64
ROWS = 256


def slot_of_tiles(irreps_ref):
    irrep = [irreps_ref[TILE * i] for i in range(TILES)]
    count = [sum((irrep[i] == g).astype(jnp.int32) for i in range(TILES)) for g in range(8)]
    three = [(c == 3).astype(jnp.int32) for c in count]
    two = [(c == 2).astype(jnp.int32) for c in count]
    one = [(c == 1).astype(jnp.int32) for c in count]
    n3, n2 = sum(three), sum(two)
    slots = [jnp.int32(0)] * TILES
    start = r3 = r2 = r1 = jnp.int32(0)
    for g in range(8):
        lone = jnp.where(r1 < n2, 3 * (n3 + r1) + 2, 3 * (n3 + n2) + r1 - n2)
        base = jnp.where(three[g] == 1, 3 * r3, jnp.where(two[g] == 1, 3 * (n3 + r2), lone))
        for i in range(TILES):
            slots[i] = jnp.where(irrep[i] == g, base + i - start, slots[i])
        start, r3, r2, r1 = start + count[g], r3 + three[g], r2 + two[g], r1 + one[g]
    return irrep, slots


def kernel(
    t_ref, v_ref, irreps_ref, out_ref,
    traw, tpart, tsend, trecv, vraw, vpack, vsend, vrecv, vall, osend, orecv, ofull,
    pick, vpick, vrow, unpick,
    send_sem, recv_sem, local_sem,
):
    pair, virt = lax.axis_index("pair"), lax.axis_index("virt")
    y, zl = pair // 4, pair % 4
    x, zh, k = virt // 4, (virt // 2) % 2, virt % 2

    def device(x=x, y=y, zh=zh, zl=zl, k=k):
        return (y * 4 + zl, (x * 2 + zh) * 2 + k)

    xs = [(x + j) % 4 for j in (1, 3, 2)]
    zs = [(zl + j) % 4 for j in (1, 2, 3)]
    up, down = (y + 1) % 8, (y + 7) % 8
    peers = (
        [device(k=1 - k), device(zh=1 - zh), device(zh=1 - zh, k=1 - k)]
        + [device(x=o) for o in xs] + [device(zl=o) for o in zs] + [device(y=up), device(y=down)]
    )
    barrier = pltpu.get_barrier_semaphore()
    for peer in peers:
        pl.semaphore_signal(barrier, inc=1, device_id=peer, device_id_type=MESH)
    pl.semaphore_wait(barrier, len(peers))

    used = [0]
    sent = []

    def send(src, dst, to):
        n = used[0]
        used[0] += 1
        copy = pltpu.make_async_remote_copy(
            src_ref=src, dst_ref=dst, send_sem=send_sem.at[n], recv_sem=recv_sem.at[n],
            device_id=to, device_id_type=MESH,
        )
        copy.start()
        sent.append(copy)
        return copy

    mine = pl.multiple_of(k * HALF, HALF)
    theirs = pl.multiple_of((1 - k) * HALF, HALF)
    vmine, vtheirs = pl.multiple_of(k * 96, 32), pl.multiple_of((1 - k) * 96, 32)
    tmine, ttheirs = pl.multiple_of(k * ROWS, ROWS), pl.multiple_of((1 - k) * ROWS, ROWS)
    other = device(k=1 - k)

    vraw_copy = send(v_ref.at[pl.ds(vtheirs, 96), :], vraw.at[:, pl.ds(mine, HALF)], other)
    own_copies, far_copies = [], []
    for j in range(CHUNKS):
        rows = pl.ds(ttheirs + j * RC, RC)
        own_copies.append(send(t_ref.at[rows, :], traw.at[0, j, :, pl.ds(mine, HALF)], other))
    for j in range(CHUNKS):
        pair_copies = []
        pair_copies.append(
            send(t_ref.at[pl.ds(tmine + j * RC, RC), :], traw.at[1, j, :, pl.ds(mine, HALF)], device(zh=1 - zh))
        )
        pair_copies.append(
            send(t_ref.at[pl.ds(ttheirs + j * RC, RC), :], traw.at[1, j, :, pl.ds(mine, HALF)],
                 device(zh=1 - zh, k=1 - k))
        )
        far_copies.append(pair_copies)
    vraw[:, pl.ds(mine, HALF)] = v_ref[pl.ds(vmine, 96), :]
    for j in range(CHUNKS):
        traw[0, j, :, pl.ds(mine, HALF)] = t_ref[pl.ds(tmine + j * RC, RC), :]

    irrep, slots = slot_of_tiles(irreps_ref)
    bins = [s // 3 for s in slots]
    places = [(s % 3) * TILE for s in slots]

    shift = (x % 2) * TILE
    diff = lax.broadcasted_iota(jnp.int32, (TILE, 1024), 1) - lax.broadcasted_iota(jnp.int32, (TILE, 1024), 0)
    for i in range(TILES):
        vpick[pl.ds(i * TILE, TILE), :] = jnp.where(diff == bins[i] * 256 + shift + places[i], 1.0, 0.0).astype(BF16)
    lane = lax.broadcasted_iota(jnp.int32, (1, 1024), 1)
    lane_irrep = jnp.full((1, 1024), -1, jnp.int32)
    for i in range(TILES):
        at = bins[i] * 256 + shift + places[i]
        lane_irrep = jnp.where((lane >= at) & (lane < at + TILE), irrep[i], lane_irrep)

    vraw_copy.wait_recv()
    packed = jnp.dot(vraw[...], vpick[...], preferred_element_type=F32)
    for j in range(3):
        row_irrep = irreps_ref[TILE * (3 * zl + (k * 3 + j) // 2)]
        part = jnp.where(lane_irrep == row_irrep, packed[j * 32:(j + 1) * 32, :], 0.0)
        part = part[:, 0:256] + part[:, 256:512] + part[:, 512:768] + part[:, 768:1024]
        vpack[zl, k, pl.ds(j * 32, 32), :] = part.astype(BF16)
    mypack = vpack.at[zl, k]
    zcopies = [send(mypack, mypack, device(zl=o)) for o in zs]
    dcopies = [send(mypack, mypack, other)]

    olane = lax.broadcasted_iota(jnp.int32, (1, NVIR), 1)
    oslot = jnp.zeros((1, NVIR), jnp.int32)
    opad = jnp.zeros((1, NVIR), jnp.int32)
    for i in range(TILES):
        here = (olane >= i * TILE) & (olane < (i + 1) * TILE)
        oslot = jnp.where(here, slots[i] * TILE + olane - i * TILE, oslot)
        opad = jnp.where(here, bins[i] * 256 + places[i] + olane - i * TILE, opad)
    for m in range(BINS):
        want = lax.broadcasted_iota(jnp.int32, (96, NVIR), 0) + m * BIN + k * 96
        vrow[pl.ds(m * 96, 96), :] = jnp.where(want == oslot, 1.0, 0.0).astype(BF16)

    for j, o in enumerate(zs):
        source = (zl + 4 - (1, 2, 3)[j]) % 4
        zcopies[j].wait_recv()
        dcopies.append(send(vpack.at[source, k], vpack.at[source, k], other))
    for copy in dcopies:
        copy.wait_recv()
    full = jnp.concatenate([vpack[z, c] for z in range(4) for c in range(2)], axis=0)
    vsend[...] = jnp.dot(vrow[...], full, preferred_element_type=F32).astype(BF16).reshape(BINS, 96, 256)
    xcopies = [send(vsend.at[o], vrecv.at[x], device(x=o)) for o in xs]
    vrecv[x] = vsend[x]

    wide = lax.broadcasted_iota(jnp.int32, (TILE, 1536), 1) - lax.broadcasted_iota(jnp.int32, (TILE, 1536), 0)
    for h in range(2):
        offset = (zh if h == 0 else 1 - zh) * BIN
        for i in range(TILES):
            pick[h, pl.ds(i * TILE, TILE), :] = jnp.where(wide == bins[i] * HALF + offset + places[i], 1.0, 0.0).astype(BF16)
    for j in range(CHUNKS):
        own_copies[j].wait_recv()
        tpart[j] = jnp.dot(traw[0, j], pick[0], preferred_element_type=F32).astype(BF16)

    for copy in xcopies:
        copy.wait_recv()
    myrows = pl.ds(vmine, 96)
    for h in range(2):
        a, b = vrecv[2 * h], vrecv[2 * h + 1]
        vall[y, myrows, pl.ds(h * HALF, 128)] = a[:, 0:128]
        vall[y, myrows, pl.ds(h * HALF + 128, 128)] = a[:, 128:256] + b[:, 0:128]
        vall[y, myrows, pl.ds(h * HALF + 256, 128)] = b[:, 128:256]
    vcore = [send(vall.at[y, myrows], vall.at[y, myrows], other)]
    ups = [send(vall.at[y, myrows], vall.at[y, myrows], device(y=up))]
    downs = [send(vall.at[y, myrows], vall.at[y, myrows], device(y=down))]

    for i in range(TILES):
        unpick_at = lax.broadcasted_iota(jnp.int32, (256, NVIR), 0)
    for m in range(BINS):
        unpick[pl.ds(m * 256, 256), :] = jnp.where(unpick_at + m * 256 == opad, 1.0, 0.0).astype(BF16)
    osend[...] = jnp.zeros_like(osend)

    tcopies = []

    def regroup(j):
        for copy in far_copies[j]:
            copy.wait_recv()
        tsend[j] = tpart[j] + jnp.dot(traw[1, j], pick[1], preferred_element_type=F32).astype(BF16)
        tcopies.append([
            send(tsend.at[j, :, pl.ds(pl.multiple_of(o * HALF, HALF), HALF)],
                 trecv.at[j, :, pl.ds(pl.multiple_of(x * HALF, HALF), HALF)], device(x=o))
            for o in xs
        ])
        own = pl.ds(pl.multiple_of(x * HALF, HALF), HALF)
        trecv[j, :, own] = tsend[j, :, own]

    for step in range(1, 5):
        from_down, from_up = (y + 8 - step) % 8, (y + step) % 8
        regroup(step - 1)
        if step < 4:
            a, b = vall.at[from_down, myrows], vall.at[from_up, myrows]
            ups[-1].wait_recv()
            if step < 3:
                ups.append(send(a, a, device(y=up)))
            else:
                a_half = vall.at[from_down, pl.ds(vmine, 48)]
                ups.append(send(a_half, a_half, device(y=up)))
            vcore.append(send(a, a, other))
            downs[-1].wait_recv()
            if step < 3:
                downs.append(send(b, b, device(y=down)))
            else:
                b_half = vall.at[from_up, pl.ds(vmine + 48, 48)]
                downs.append(send(b_half, b_half, device(y=down)))
            vcore.append(send(b, b, other))
        else:
            ups[-1].wait_recv()
            downs[-1].wait_recv()
            last = vall.at[from_down, myrows]
            vcore.append(send(last, last, other))
    for copy in vcore:
        copy.wait_recv()

    ocopies = []
    for j in range(CHUNKS):
        for copy in tcopies[j]:
            copy.wait_recv()
        total = jnp.dot(trecv[j], vall[...].reshape(8 * BIN, NVIR), preferred_element_type=F32)
        for a in range(4):
            osend[j, :, pl.ds(a * 256, BIN)] = total[:, a * BIN:(a + 1) * BIN].astype(BF16)
        ocopies.append([
            send(osend.at[j, :, pl.ds(pl.multiple_of(o * 256, 256), 256)],
                 orecv.at[j, :, pl.ds(pl.multiple_of(x * 256, 256), 256)], device(x=o))
            for o in xs
        ])
        own = pl.ds(pl.multiple_of(x * 256, 256), 256)
        orecv[j, :, own] = osend[j, :, own]
    last_copies, locals_ = [], []
    for j in range(CHUNKS):
        for copy in ocopies[j]:
            copy.wait_recv()
        ofull[j] = jnp.dot(orecv[j], unpick[...], preferred_element_type=F32).astype(BF16)
        rows = pl.ds(tmine + j * RC, RC)
        last_copies.append(send(ofull.at[j, :, pl.ds(theirs, HALF)], out_ref.at[rows, :], other))
        local = pltpu.make_async_copy(ofull.at[j, :, pl.ds(mine, HALF)], out_ref.at[rows, :], local_sem.at[j])
        local.start()
        locals_.append(local)
    for copy in last_copies:
        copy.wait_recv()
    for copy in locals_:
        copy.wait()
    for copy in sent:
        copy.wait_send()


SEMS = 80


def binned(amplitudes, integrals, irreps):
    vmem = lambda *shape: pltpu.VMEM(shape, BF16)
    return pl.pallas_call(
        kernel,
        out_shape=jax.ShapeDtypeStruct((512, HALF), BF16),
        in_specs=[
            pl.BlockSpec(memory_space=pltpu.VMEM), pl.BlockSpec(memory_space=pltpu.VMEM),
            pl.BlockSpec(memory_space=pltpu.SMEM),
        ],
        out_specs=pl.BlockSpec(memory_space=pl.ANY),
        scratch_shapes=[
            vmem(2, CHUNKS, RC, NVIR), vmem(CHUNKS, RC, 1536), vmem(CHUNKS, RC, 1536), vmem(CHUNKS, RC, 1536),
            vmem(96, NVIR), vmem(4, 2, 96, 256), vmem(BINS, 96, 256), vmem(4, 96, 256), vmem(8, BIN, NVIR),
            vmem(CHUNKS, RC, 1024), vmem(CHUNKS, RC, 1024), vmem(CHUNKS, RC, NVIR),
            vmem(2, NVIR, 1536), vmem(NVIR, 1024), vmem(HALF, NVIR), vmem(1024, NVIR),
            pltpu.SemaphoreType.DMA((SEMS,)), pltpu.SemaphoreType.DMA((SEMS,)), pltpu.SemaphoreType.DMA((CHUNKS,)),
        ],
        compiler_params=pltpu.CompilerParams(collective_id=0, has_side_effects=True, vmem_limit_bytes=48 << 20),
        name="ladder",
    )(amplitudes, integrals, irreps)


def gathered(amplitudes, integrals, irreps):
    col_first = (lax.axis_index("virt") % 2) * HALF
    col_sym = lax.dynamic_slice_in_dim(irreps, col_first, HALF, 0)
    row_sym = jnp.tile(irreps, 8)
    every = lax.all_gather(amplitudes, "virt", axis=1, tiled=True)
    slab = lax.all_gather(integrals, "pair", axis=0, tiled=True)
    masked = jnp.where(row_sym[:, None] == col_sym[None, :], slab, jnp.zeros_like(slab))
    return jnp.dot(every, masked, preferred_element_type=F32).astype(BF16)


def per_device(amplitudes, integrals, irreps):
    tiles = irreps.reshape(TILES, TILE)[:, 0]
    wide = jnp.any(tiles[:-3] == tiles[3:])
    return lax.cond(wide, gathered, binned, amplitudes, integrals, irreps)


def solution(mesh):
    placed = (P("pair", "virt"), P("pair", "virt"), P())
    return jax.shard_map(
        per_device, mesh=mesh, in_specs=placed, out_specs=P("pair", "virt"), check_vma=False
    )
```

time: 297 us -> 92.3 us (0.31)
  waiting for transfers between devices: 274 us -> 0 us
  Pallas kernels: 0 us -> 75.9 us
  matrix products: 6.99 us -> 0 us
    all_gather x2 -> x0, waiting for transfers between devices: 273 us -> none  [the longest x1 147 us: per_device(): slab_part = lax.all_gather(integrals, 'pair', axis=0, tiled=True)]
    pallas_call x0 -> x1, Pallas kernels: none -> 75.9 us  [binned(): pl.pallas_call(kernel, out_shape=jax.ShapeDtypeStruct((512, HALF), BF16),...]
    dot_general x1 -> x0, matrix products: 6.99 us -> none  [per_device(): ladder = jnp.dot(gathered, masked, preferred_element_type=jnp.float32)]
  transfers between devices with their start and end apart: 2 -> 0, of which waited for: 2 -> 0; matrix products, arithmetic and copies ran while one was open for 1% -> 0% of each run, Pallas kernels for 0% -> 0%
where the time goes in v1:
time: 92.3 us; the launch traced here: 92.1 us
  Pallas kernels  75.9 us (82%)
  between operations  14 us (15%)
  local copies, waits for them, and re-layouts  1.5 us (2%)
    pallas_call x1, Pallas kernels, binned(): pl.pallas_call(kernel, out_shape=jax.ShapeDtypeStruct((512, HALF), BF16),...  75.9 us

profile of v1, /device:TPU:1, one launch (start us, length us, event | category | flops | bytes accessed | tf_op | source)
XLA Modules:
  0.0 92.1 jit_solution(4792638059350520002)
XLA Ops:
  6.5 0.8 reshape.9
  7.3 0.6 fusion.7
  8.6 75.9 %conditional.1 = (bf16[512,384]{1,0:T(8,128)(2,1)S(1)}) conditional(s32[]{:T(128)} %convert_element_type.9, (bf16[512,384]{1,0:T(8,128)(2,1)}, bf16[192,384]{1,0:T(8,128)(2,1)}, s32[768]{0:T(1024)}) %tuple.11, (s32[768]{0:T(1024)}, bf16[192,384]{1,0:T(8,128)(2,1)}, bf16[512,384]{1,0:T(8,128)(2,1)}) %tuple.12), branch_computations={%region_1.0_spmd, %region_2.3_spmd} | conditional | flops 2420834304 | bytes 46948100 | solution.py:289
  8.6 75.9 %ladder.1 = bf16[512,384]{1,0:T(8,128)(2,1)S(1)} custom-call(bf16[512,384]{1,0:T(8,128)(2,1)} %get-tuple-element.20.t_ref, bf16[192,384]{1,0:T(8,128)(2,1)} %get-tuple-element.21.v_ref, s32[768]{0:T(1024)} %get-tuple-element.22.irreps_ref), custom_call_target="tpu_custom_call" | custom-call | tf_op jit(solution)/shard_map/cond/branch_0_fun/ladder/pallas_call | solution.py:256
  84.5 0.7 copy.19

commit v2 on v0

v2 whole, which is shorter than its diff:
```python
import functools

import jax
import jax.numpy as jnp
from jax import lax
from jax.experimental import pallas as pl
from jax.experimental.pallas import tpu as pltpu
from jax.sharding import PartitionSpec as P

MESH = pl.DeviceIdType.MESH
BF16 = jnp.bfloat16
F32 = jnp.float32
TILE = 64
TILES = 12
BINS = 4
NVIR = 768
HALF = 384
CHUNKS = 4
ROWS = 256
RC = ROWS // CHUNKS
SEMS = 80


def places_of_tiles(irreps_ref):
    irrep = [irreps_ref[TILE * i] for i in range(TILES)]
    count = [sum((irrep[i] == g).astype(jnp.int32) for i in range(TILES)) for g in range(8)]
    big = [(c >= 3).astype(jnp.int32) for c in count]
    two = [(c == 2).astype(jnp.int32) for c in count]
    one = [(c == 1).astype(jnp.int32) for c in count]
    n3, n2 = sum(big), sum(two)
    bins, places = [jnp.int32(0)] * TILES, [jnp.int32(0)] * TILES
    start = r3 = r2 = r1 = jnp.int32(0)
    for g in range(8):
        lone = jnp.where(r1 < n2, 3 * (n3 + r1) + 2, 3 * (n3 + n2) + r1 - n2)
        base = jnp.where(big[g] == 1, 3 * r3, jnp.where(two[g] == 1, 3 * (n3 + r2), lone))
        for i in range(TILES):
            here = irrep[i] == g
            bins[i] = jnp.where(here, base // 3, bins[i])
            places[i] = jnp.where(here, (base % 3 + i - start) * TILE, places[i])
        start, r3, r2, r1 = start + count[g], r3 + big[g], r2 + two[g], r1 + one[g]
    return irrep, bins, places


def kernel(
    W, t_ref, v_ref, irreps_ref, out_ref,
    traw, tpart, tsend, trecv, vraw, vpack, vsend, vrecv, vall, osend, orecv, ofull,
    pick, vpick, vrow, unpick,
    send_sem, recv_sem, local_sem,
):
    PW, W2, H = W + 64, 2 * W, W // 2
    pair, virt = lax.axis_index("pair"), lax.axis_index("virt")
    y, zl = pair // 4, pair % 4
    x, zh, k = virt // 4, (virt // 2) % 2, virt % 2

    def device(x=x, y=y, zh=zh, zl=zl, k=k):
        return (y * 4 + zl, (x * 2 + zh) * 2 + k)

    near = x + 1 - 2 * (x % 2)
    own2, far2 = x // 2, 1 - x // 2
    xs = [(x + j) % 4 for j in (1, 3, 2)]
    zs = [(zl + j) % 4 for j in (1, 2, 3)]
    up, down = (y + 1) % 8, (y + 7) % 8
    peers = (
        [device(k=1 - k), device(zh=1 - zh), device(zh=1 - zh, k=1 - k)]
        + [device(x=o) for o in xs] + [device(zl=o) for o in zs] + [device(y=up), device(y=down)]
    )
    barrier = pltpu.get_barrier_semaphore()
    for peer in peers:
        pl.semaphore_signal(barrier, inc=1, device_id=peer, device_id_type=MESH)

    mine = pl.multiple_of(k * HALF, HALF)
    theirs = pl.multiple_of((1 - k) * HALF, HALF)
    vmine, vtheirs = pl.multiple_of(k * 96, 32), pl.multiple_of((1 - k) * 96, 32)
    tmine, ttheirs = pl.multiple_of(k * ROWS, ROWS), pl.multiple_of((1 - k) * ROWS, ROWS)
    other = device(k=1 - k)

    vown = pltpu.make_async_copy(v_ref.at[pl.ds(vmine, 96), :], vraw.at[:, pl.ds(mine, HALF)], local_sem.at[0])
    vown.start()
    town = pltpu.make_async_copy(t_ref.at[pl.ds(tmine, ROWS), :], traw.at[0, :, pl.ds(mine, HALF)], local_sem.at[1])
    town.start()

    irrep, bins, places = places_of_tiles(irreps_ref)
    shift = (x % 2) * TILE
    padded = [bins[i] * PW + shift + places[i] for i in range(TILES)]

    diff = lax.broadcasted_iota(jnp.int32, (TILE, 4 * PW), 1) - lax.broadcasted_iota(jnp.int32, (TILE, 4 * PW), 0)
    for i in range(TILES):
        vpick[pl.ds(i * TILE, TILE), :] = jnp.where(diff == padded[i], 1.0, 0.0).astype(BF16)
    lane = lax.broadcasted_iota(jnp.int32, (1, 4 * PW), 1)
    lane_irrep = jnp.full((1, 4 * PW), -1, jnp.int32)
    for i in range(TILES):
        lane_irrep = jnp.where((lane >= padded[i]) & (lane < padded[i] + TILE), irrep[i], lane_irrep)

    pl.semaphore_wait(barrier, len(peers))

    used = [0]
    sent = []

    def send(src, dst, to):
        n = used[0]
        used[0] += 1
        copy = pltpu.make_async_remote_copy(
            src_ref=src, dst_ref=dst, send_sem=send_sem.at[n], recv_sem=recv_sem.at[n],
            device_id=to, device_id_type=MESH,
        )
        copy.start()
        sent.append(copy)
        return copy

    far_copies = []

    def send_far(j):
        lanes = pl.ds(mine, HALF)
        dst = traw.at[1, pl.ds(j * RC, RC), lanes]
        far_copies.append([
            send(t_ref.at[pl.ds(tmine + j * RC, RC), :], dst, device(zh=1 - zh)),
            send(t_ref.at[pl.ds(ttheirs + j * RC, RC), :], dst, device(zh=1 - zh, k=1 - k)),
        ])

    vraw_copy = send(v_ref.at[pl.ds(vtheirs, 96), :], vraw.at[:, pl.ds(mine, HALF)], other)
    send_far(0)
    traw_copy = send(t_ref.at[pl.ds(ttheirs, ROWS), :], traw.at[0, :, pl.ds(mine, HALF)], other)

    vown.wait()
    vraw_copy.wait_recv()
    packed = jnp.dot(vraw[...], vpick[...], preferred_element_type=F32)
    for j in range(3):
        row_irrep = irreps_ref[TILE * (3 * zl + (k * 3 + j) // 2)]
        part = jnp.where(lane_irrep == row_irrep, packed[j * 32:(j + 1) * 32, :], 0.0)
        part = part[:, 0:PW] + part[:, PW:2 * PW] + part[:, 2 * PW:3 * PW] + part[:, 3 * PW:4 * PW]
        vpack[zl, k, pl.ds(j * 32, 32), :] = part.astype(BF16)
    mypack = vpack.at[zl, k]
    zcopies = [send(mypack, mypack, device(zl=o)) for o in zs]
    dcopies = [send(mypack, mypack, other)]
    for j in range(1, CHUNKS):
        send_far(j)

    olane = lax.broadcasted_iota(jnp.int32, (1, NVIR), 1)
    oslot = jnp.zeros((1, NVIR), jnp.int32)
    opad = jnp.zeros((1, NVIR), jnp.int32)
    for i in range(TILES):
        here = (olane >= i * TILE) & (olane < (i + 1) * TILE)
        oslot = jnp.where(here, bins[i] * W + places[i] + olane - i * TILE, oslot)
        opad = jnp.where(here, padded[i] + olane - i * TILE, opad)
    for m in range(BINS):
        want = lax.broadcasted_iota(jnp.int32, (H, NVIR), 0) + m * W + k * H
        vrow[pl.ds(m * H, H), :] = jnp.where(want == oslot, 1.0, 0.0).astype(BF16)

    wide = lax.broadcasted_iota(jnp.int32, (TILE, 4 * W2), 1) - lax.broadcasted_iota(jnp.int32, (TILE, 4 * W2), 0)
    for h in range(2):
        offset = (zh if h == 0 else 1 - zh) * W
        for i in range(TILES):
            pick[h, pl.ds(i * TILE, TILE), :] = jnp.where(wide == bins[i] * W2 + offset + places[i], 1.0, 0.0).astype(BF16)

    for j, o in enumerate(zs):
        source = (zl + 4 - (1, 2, 3)[j]) % 4
        zcopies[j].wait_recv()
        dcopies.append(send(vpack.at[source, k], vpack.at[source, k], other))

    town.wait()
    traw_copy.wait_recv()
    tpart[...] = jnp.dot(traw[0], pick[0], preferred_element_type=F32).astype(BF16)

    for copy in dcopies:
        copy.wait_recv()
    full = jnp.concatenate([vpack[z, c] for z in range(4) for c in range(2)], axis=0)
    vsend[...] = jnp.dot(vrow[...], full, preferred_element_type=F32).astype(BF16).reshape(BINS, H, PW)
    xcopies = [send(vsend.at[o], vrecv.at[x], device(x=o)) for o in xs]
    vrecv[x] = vsend[x]

    tcopies = []

    def regroup(j):
        rows = pl.ds(j * RC, RC)
        for copy in far_copies[j]:
            copy.wait_recv()
        tsend[rows, :] = tpart[rows, :] + jnp.dot(traw[1, rows, :], pick[1], preferred_element_type=F32).astype(BF16)
        own = pl.ds(pl.multiple_of(x * W2, W2), W2)
        tcopies.append([
            send(tsend.at[rows, pl.ds(pl.multiple_of(o * W2, W2), W2)], trecv.at[rows, own], device(x=o)) for o in xs
        ])
        trecv[rows, own] = tsend[rows, own]

    regroup(0)

    for copy in xcopies:
        copy.wait_recv()
    myrows = pl.ds(pl.multiple_of(k * H, 16), H)
    pairs = [pl.ds(pl.multiple_of(p * W2, W2), W2) for p in (far2, own2)]
    vcore, ups, downs = [], [[], []], [[], []]

    def share(ref):
        vcore.append(send(ref, ref, other))

    for p, q in enumerate((far2, own2)):
        a, b = vrecv[2 * q], vrecv[2 * q + 1]
        merged = jnp.concatenate([a[:, :W - 64], a[:, W - 64:] + b[:, :128], b[:, 128:]], axis=1)
        vall[y, myrows, pairs[p]] = merged
        piece = vall.at[y, myrows, pairs[p]]
        ups[p].append(send(piece, piece, device(y=up)))
        downs[p].append(send(piece, piece, device(y=down)))
        share(piece)

    unpick_at = lax.broadcasted_iota(jnp.int32, (PW, NVIR), 0)
    for m in range(BINS):
        unpick[pl.ds(m * PW, PW), :] = jnp.where(unpick_at + m * PW == opad, 1.0, 0.0).astype(BF16)

    regroup(1)

    def relay(step, p):
        from_down, from_up = (y + 8 - step) % 8, (y + step) % 8
        a, b = vall.at[from_down, myrows, pairs[p]], vall.at[from_up, myrows, pairs[p]]
        ups[p][-1].wait_recv()
        if step == 4:
            downs[p][-1].wait_recv()
            share(a)
            return
        if step < 3:
            ups[p].append(send(a, a, device(y=up)))
        else:
            half = vall.at[from_down, pl.ds(pl.multiple_of(k * H, 16), H // 2), pairs[p]]
            ups[p].append(send(half, half, device(y=up)))
        downs[p][-1].wait_recv()
        if step < 3:
            downs[p].append(send(b, b, device(y=down)))
        else:
            half = vall.at[from_up, pl.ds(pl.multiple_of(k * H + H // 2, 16), H // 2), pairs[p]]
            downs[p].append(send(half, half, device(y=down)))
        share(a)
        share(b)

    relay(1, 0)
    relay(1, 1)
    regroup(2)
    relay(2, 0)
    relay(2, 1)
    regroup(3)
    relay(3, 0)
    relay(3, 1)
    relay(4, 0)
    for copies in tcopies:
        for copy in copies:
            copy.wait_recv()

    ocopies = []
    into = pl.ds(pl.multiple_of(x * PW, 128), PW)

    def multiply(p):
        while vcore and vcore[0] is not None:
            vcore.pop(0).wait_recv()
        total = jnp.dot(trecv[...], vall[:, :, pairs[p]].reshape(8 * W, W2), preferred_element_type=F32)
        osend[p] = total.astype(BF16)

    same = pl.multiple_of((x % 2) * (W2 - PW), 128)
    swap = pl.multiple_of((1 - x % 2) * (W2 - PW), 128)
    multiply(0)
    ocopies.append(send(osend.at[0, :, pl.ds(same, PW)], orecv.at[:, into], device(x=2 * far2 + x % 2)))
    ocopies.append(send(osend.at[0, :, pl.ds(swap, PW)], orecv.at[:, into], device(x=2 * far2 + 1 - x % 2)))
    relay(4, 1)
    multiply(1)
    halves = []
    for h in range(2):
        rows = pl.ds(h * 128, 128)
        halves.append(send(osend.at[1, rows, pl.ds(swap, PW)], orecv.at[rows, into], device(x=near)))
    orecv[:, into] = osend[1, :, pl.ds(same, PW)]
    for copy in ocopies:
        copy.wait_recv()
    last, locals_ = [], []
    for h in range(2):
        rows = pl.ds(h * 128, 128)
        halves[h].wait_recv()
        ofull[rows, :] = jnp.dot(orecv[rows, :], unpick[...], preferred_element_type=F32).astype(BF16)
        to = pl.ds(tmine + h * 128, 128)
        last.append(send(ofull.at[rows, pl.ds(theirs, HALF)], out_ref.at[to, :], other))
        local = pltpu.make_async_copy(ofull.at[rows, pl.ds(mine, HALF)], out_ref.at[to, :], local_sem.at[2 + h])
        local.start()
        locals_.append(local)
    for copy in last:
        copy.wait_recv()
    for copy in locals_:
        copy.wait()
    for copy in sent:
        copy.wait_send()


def ladder(width, amplitudes, integrals, irreps):
    vmem = lambda *shape: pltpu.VMEM(shape, BF16)
    W, PW, W2, H = width, width + 64, 2 * width, width // 2
    return pl.pallas_call(
        functools.partial(kernel, W),
        out_shape=jax.ShapeDtypeStruct((512, HALF), BF16),
        in_specs=[
            pl.BlockSpec(memory_space=pl.ANY), pl.BlockSpec(memory_space=pl.ANY),
            pl.BlockSpec(memory_space=pltpu.SMEM),
        ],
        out_specs=pl.BlockSpec(memory_space=pl.ANY),
        scratch_shapes=[
            vmem(2, ROWS, NVIR), vmem(ROWS, 4 * W2), vmem(ROWS, 4 * W2), vmem(ROWS, 4 * W2),
            vmem(96, NVIR), vmem(4, 2, 96, PW), vmem(BINS, H, PW), vmem(4, H, PW), vmem(8, W, 4 * W),
            vmem(2, ROWS, W2), vmem(ROWS, 4 * PW), vmem(ROWS, NVIR),
            vmem(2, NVIR, 4 * W2), vmem(NVIR, 4 * PW), vmem(4 * H, NVIR), vmem(4 * PW, NVIR),
            pltpu.SemaphoreType.DMA((SEMS,)), pltpu.SemaphoreType.DMA((SEMS,)), pltpu.SemaphoreType.DMA((4,)),
        ],
        compiler_params=pltpu.CompilerParams(
            collective_id=width // 300, has_side_effects=True, vmem_limit_bytes=56 << 20
        ),
        name="ladder%d" % width,
    )(amplitudes, integrals, irreps)


def per_device(amplitudes, integrals, irreps):
    wide = jnp.any(irreps[:-192] == irreps[192:])
    return lax.cond(
        wide, functools.partial(ladder, 320), functools.partial(ladder, 192), amplitudes, integrals, irreps
    )


def solution(mesh):
    placed = (P("pair", "virt"), P("pair", "virt"), P())
    return jax.shard_map(
        per_device, mesh=mesh, in_specs=placed, out_specs=P("pair", "virt"), check_vma=False
    )
```

time: 297 us -> 75.3 us (0.25)
  waiting for transfers between devices: 274 us -> 0 us
  Pallas kernels: 0 us -> 71.5 us
  between operations: 13.4 us -> 0.67 us
  matrix products: 6.99 us -> 0 us
    all_gather x2 -> x0, waiting for transfers between devices: 273 us -> none  [the longest x1 147 us: per_device(): slab_part = lax.all_gather(integrals, 'pair', axis=0, tiled=True)]
    pallas_call x0 -> x1, Pallas kernels: none -> 71.5 us  [ladder(): pl.pallas_call(functools.partial(kernel, W), out_shape=jax.ShapeDtypeStru...]
    dot_general x1 -> x0, matrix products: 6.99 us -> none  [per_device(): ladder = jnp.dot(gathered, masked, preferred_element_type=jnp.float32)]
  transfers between devices with their start and end apart: 2 -> 0, of which waited for: 2 -> 0; matrix products, arithmetic and copies ran while one was open for 1% -> 0% of each run, Pallas kernels for 0% -> 0%
where the time goes in v2:
time: 75.3 us; the launch traced here: 74.7 us
  Pallas kernels  71.5 us (95%)
  other arithmetic  1.5 us (2%)
    pallas_call x1, Pallas kernels, ladder(): pl.pallas_call(functools.partial(kernel, W), out_shape=jax.ShapeDtypeStru...  71.5 us

profile of v2, /device:TPU:1, one launch (start us, length us, event | category | flops | bytes accessed | tf_op | source)
XLA Modules:
  0.0 74.7 jit_solution(17028608284312164861)
XLA Ops:
  0.0 0.0 copy-start
  0.0 1.5 %fusion = pred[]{:T(512)} fusion(s32[768]{0:T(1024)} %param.7), kind=kLoop, calls=%fused_computation.1 | loop fusion | flops 1151 | bytes 4609 | tf_op jit(solution)/shard_map/reduce_or | solution.py:312
  2.2 0.0 copy-done
  2.2 71.7 %conditional.1 = (bf16[512,384]{1,0:T(8,128)(2,1)S(1)}) conditional(s32[]{:T(128)} %convert_element_type.3, (bf16[512,384]{1,0:T(8,128)(2,1)}, bf16[192,384]{1,0:T(8,128)(2,1)}, s32[768]{0:T(1024)S(1)}) %tuple.16, (bf16[512,384]{1,0:T(8,128)(2,1)}, bf16[192,384]{1,0:T(8,128)(2,1)}, s32[768]{0:T(1024)S(1)}) %tuple.17), branch_computations={%region_1.0_spmd, %region_2.0_spmd} | conditional | bytes 8 | solution.py:313
  2.2 71.5 %ladder192.1 = bf16[512,384]{1,0:T(8,128)(2,1)S(1)} custom-call(bf16[512,384]{1,0:T(8,128)(2,1)} %get-tuple-element.31.t_ref, bf16[192,384]{1,0:T(8,128)(2,1)} %get-tuple-element.33.v_ref, s32[768]{0:T(1024)S(1)} %get-tuple-element.22.irreps_ref), custom_call_target="tpu_custom_call" | custom-call | tf_op jit(solution)/shard_map/cond/branch_0_fun/ladder192/pallas_call | solution.py:289
  73.9 0.7 %copy.13 = bf16[512,384]{1,0:T(8,128)(2,1)} copy(bf16[512,384]{1,0:T(8,128)(2,1)S(1)} %get-tuple-element.26) | data formatting | bytes 786432
Async XLA Ops:
  0.0 2.2 %copy-start = (s32[768]{0:T(1024)S(1)}, s32[768]{0:T(1024)}, u32[]{:S(2)}) copy-start(s32[768]{0:T(1024)} %param.7) | copy-start | bytes 9220

commit v3 on v2

--- a/solution.py
+++ b/solution.py
@@ -15,10 +15,9 @@
 BINS = 4
 NVIR = 768
 HALF = 384
-CHUNKS = 4
 ROWS = 256
-RC = ROWS // CHUNKS
-SEMS = 80
+CHUNKS = ((0, 32), (32, 32), (64, 64), (128, 64), (192, 64))
+SEMS = 128
 
 
 def places_of_tiles(irreps_ref):
@@ -57,7 +56,7 @@
 
     near = x + 1 - 2 * (x % 2)
     own2, far2 = x // 2, 1 - x // 2
-    xs = [(x + j) % 4 for j in (1, 3, 2)]
+    xs = [(x + j) % 4 for j in (2, 1, 3)]
     zs = [(zl + j) % 4 for j in (1, 2, 3)]
     up, down = (y + 1) % 8, (y + 7) % 8
     peers = (
@@ -110,15 +109,14 @@
     far_copies = []
 
     def send_far(j):
-        lanes = pl.ds(mine, HALF)
-        dst = traw.at[1, pl.ds(j * RC, RC), lanes]
+        first, count = CHUNKS[j]
+        dst = traw.at[1, pl.ds(first, count), pl.ds(mine, HALF)]
         far_copies.append([
-            send(t_ref.at[pl.ds(tmine + j * RC, RC), :], dst, device(zh=1 - zh)),
-            send(t_ref.at[pl.ds(ttheirs + j * RC, RC), :], dst, device(zh=1 - zh, k=1 - k)),
+            send(t_ref.at[pl.ds(tmine + first, count), :], dst, device(zh=1 - zh)),
+            send(t_ref.at[pl.ds(ttheirs + first, count), :], dst, device(zh=1 - zh, k=1 - k)),
         ])
 
     vraw_copy = send(v_ref.at[pl.ds(vtheirs, 96), :], vraw.at[:, pl.ds(mine, HALF)], other)
-    send_far(0)
     traw_copy = send(t_ref.at[pl.ds(ttheirs, ROWS), :], traw.at[0, :, pl.ds(mine, HALF)], other)
 
     vown.wait()
@@ -132,8 +130,6 @@
     mypack = vpack.at[zl, k]
     zcopies = [send(mypack, mypack, device(zl=o)) for o in zs]
     dcopies = [send(mypack, mypack, other)]
-    for j in range(1, CHUNKS):
-        send_far(j)
 
     olane = lax.broadcasted_iota(jnp.int32, (1, NVIR), 1)
     oslot = jnp.zeros((1, NVIR), jnp.int32)
@@ -156,6 +152,8 @@
         source = (zl + 4 - (1, 2, 3)[j]) % 4
         zcopies[j].wait_recv()
         dcopies.append(send(vpack.at[source, k], vpack.at[source, k], other))
+    for j in range(len(CHUNKS)):
+        send_far(j)
 
     town.wait()
     traw_copy.wait_recv()
@@ -171,7 +169,7 @@
     tcopies = []
 
     def regroup(j):
-        rows = pl.ds(j * RC, RC)
+        rows = pl.ds(*CHUNKS[j])
         for copy in far_copies[j]:
             copy.wait_recv()
         tsend[rows, :] = tpart[rows, :] + jnp.dot(traw[1, rows, :], pick[1], preferred_element_type=F32).astype(BF16)
@@ -181,88 +179,99 @@
         ])
         trecv[rows, own] = tsend[rows, own]
 
-    regroup(0)
-
     for copy in xcopies:
         copy.wait_recv()
     myrows = pl.ds(pl.multiple_of(k * H, 16), H)
-    pairs = [pl.ds(pl.multiple_of(p * W2, W2), W2) for p in (far2, own2)]
-    vcore, ups, downs = [], [[], []], [[], []]
-
-    def share(ref):
-        vcore.append(send(ref, ref, other))
-
-    for p, q in enumerate((far2, own2)):
+    same = pl.multiple_of((x % 2) * (W2 - PW), 128)
+    swap = pl.multiple_of((1 - x % 2) * (W2 - PW), 128)
+    far_lane, own_lane = far2 * W2, own2 * W2
+    pieces = [
+        pl.ds(pl.multiple_of(far_lane, 128), PW),
+        pl.ds(pl.multiple_of(far_lane + PW, 128), W2 - PW),
+        pl.ds(pl.multiple_of(own_lane + swap, 128), PW),
+        pl.ds(pl.multiple_of(own_lane + (x % 2) * PW, 128), W2 - PW),
+    ]
+    vcore, ups, downs = [[], [], [], []], [[], [], [], []], [[], [], [], []]
+
+    def share(p, ref):
+        vcore[p].append(send(ref, ref, other))
+
+    for q in (far2, own2):
         a, b = vrecv[2 * q], vrecv[2 * q + 1]
         merged = jnp.concatenate([a[:, :W - 64], a[:, W - 64:] + b[:, :128], b[:, 128:]], axis=1)
-        vall[y, myrows, pairs[p]] = merged
-        piece = vall.at[y, myrows, pairs[p]]
+        vall[y, myrows, pl.ds(pl.multiple_of(q * W2, 128), W2)] = merged
+    for p in range(4):
+        piece = vall.at[y, myrows, pieces[p]]
         ups[p].append(send(piece, piece, device(y=up)))
         downs[p].append(send(piece, piece, device(y=down)))
-        share(piece)
+    for p in range(4):
+        share(p, vall.at[y, myrows, pieces[p]])
 
     unpick_at = lax.broadcasted_iota(jnp.int32, (PW, NVIR), 0)
     for m in range(BINS):
         unpick[pl.ds(m * PW, PW), :] = jnp.where(unpick_at + m * PW == opad, 1.0, 0.0).astype(BF16)
 
-    regroup(1)
-
     def relay(step, p):
         from_down, from_up = (y + 8 - step) % 8, (y + step) % 8
-        a, b = vall.at[from_down, myrows, pairs[p]], vall.at[from_up, myrows, pairs[p]]
+        a, b = vall.at[from_down, myrows, pieces[p]], vall.at[from_up, myrows, pieces[p]]
         ups[p][-1].wait_recv()
         if step == 4:
             downs[p][-1].wait_recv()
-            share(a)
+            share(p, a)
             return
         if step < 3:
             ups[p].append(send(a, a, device(y=up)))
         else:
-            half = vall.at[from_down, pl.ds(pl.multiple_of(k * H, 16), H // 2), pairs[p]]
+            half = vall.at[from_down, pl.ds(pl.multiple_of(k * H, 16), H // 2), pieces[p]]
             ups[p].append(send(half, half, device(y=up)))
         downs[p][-1].wait_recv()
         if step < 3:
             downs[p].append(send(b, b, device(y=down)))
         else:
-            half = vall.at[from_up, pl.ds(pl.multiple_of(k * H + H // 2, 16), H // 2), pairs[p]]
+            half = vall.at[from_up, pl.ds(pl.multiple_of(k * H + H // 2, 16), H // 2), pieces[p]]
             downs[p].append(send(half, half, device(y=down)))
-        share(a)
-        share(b)
-
-    relay(1, 0)
-    relay(1, 1)
-    regroup(2)
-    relay(2, 0)
-    relay(2, 1)
-    regroup(3)
-    relay(3, 0)
-    relay(3, 1)
+        share(p, a)
+        share(p, b)
+
+    regroup(0)
+    regroup(1)
+    for step in range(1, 4):
+        for p in range(4):
+            relay(step, p)
+        regroup(step + 1)
     relay(4, 0)
+    relay(4, 1)
     for copies in tcopies:
         for copy in copies:
             copy.wait_recv()
 
-    ocopies = []
     into = pl.ds(pl.multiple_of(x * PW, 128), PW)
 
-    def multiply(p):
-        while vcore and vcore[0] is not None:
-            vcore.pop(0).wait_recv()
-        total = jnp.dot(trecv[...], vall[:, :, pairs[p]].reshape(8 * W, W2), preferred_element_type=F32)
-        osend[p] = total.astype(BF16)
-
-    same = pl.multiple_of((x % 2) * (W2 - PW), 128)
-    swap = pl.multiple_of((1 - x % 2) * (W2 - PW), 128)
-    multiply(0)
-    ocopies.append(send(osend.at[0, :, pl.ds(same, PW)], orecv.at[:, into], device(x=2 * far2 + x % 2)))
-    ocopies.append(send(osend.at[0, :, pl.ds(swap, PW)], orecv.at[:, into], device(x=2 * far2 + 1 - x % 2)))
-    relay(4, 1)
-    multiply(1)
+    def multiply(rows, lanes):
+        block = vall[:, :, lanes].reshape(8 * W, lanes.size)
+        return jnp.dot(trecv[rows, :], block, preferred_element_type=F32).astype(BF16)
+
+    def arrived(*which):
+        for p in which:
+            for copy in vcore[p]:
+                copy.wait_recv()
+
+    arrived(0, 1)
+    osend[0] = multiply(pl.ds(0, ROWS), pl.ds(pl.multiple_of(far_lane, 128), W2))
+    ocopies = [
+        send(osend.at[0, :, pl.ds(same, PW)], orecv.at[:, into], device(x=2 * far2 + x % 2)),
+        send(osend.at[0, :, pl.ds(swap, PW)], orecv.at[:, into], device(x=2 * far2 + 1 - x % 2)),
+    ]
+    relay(4, 2)
+    relay(4, 3)
+    arrived(2)
     halves = []
     for h in range(2):
         rows = pl.ds(h * 128, 128)
-        halves.append(send(osend.at[1, rows, pl.ds(swap, PW)], orecv.at[rows, into], device(x=near)))
-    orecv[:, into] = osend[1, :, pl.ds(same, PW)]
+        osend[1, rows, pl.ds(0, PW)] = multiply(rows, pieces[2])
+        halves.append(send(osend.at[1, rows, pl.ds(0, PW)], orecv.at[rows, into], device(x=near)))
+    arrived(3)
+    orecv[:, into] = multiply(pl.ds(0, ROWS), pl.ds(pl.multiple_of(own_lane + same, 128), PW))
     for copy in ocopies:
         copy.wait_recv()
     last, locals_ = [], []

time: 75.3 us -> 61.9 us (0.82)
  Pallas kernels: 71.5 us -> 58.5 us
    pallas_call x1, Pallas kernels: 71.5 us -> 58.5 us  [ladder(): pl.pallas_call(functools.partial(kernel, W), out_shape=jax.ShapeDtypeStru...]
where the time goes in v3:
time: 61.9 us; the launch traced here: 61.6 us
  Pallas kernels  58.5 us (95%)
  other arithmetic  1.5 us (2%)
  local copies, waits for them, and re-layouts  0.75 us (1%)
  between operations  0.67 us (1%)
    pallas_call x1, Pallas kernels, ladder(): pl.pallas_call(functools.partial(kernel, W), out_shape=jax.ShapeDtypeStru...  58.5 us
    reduce_or x1, other arithmetic, per_device(): wide = jnp.any(irreps[:-192] == irreps[192:])  1.5 us

profile of v3, /device:TPU:1, one launch (start us, length us, event | category | flops | bytes accessed | tf_op | source)
XLA Modules:
  0.0 61.6 jit_solution(5271572333212885501)
XLA Ops:
  0.0 0.0 copy-start
  0.0 1.5 %fusion = pred[]{:T(512)} fusion(s32[768]{0:T(1024)} %param.7), kind=kLoop, calls=%fused_computation.1 | loop fusion | flops 1151 | bytes 4609 | tf_op jit(solution)/shard_map/reduce_or | solution.py:321
  2.2 0.0 copy-done
  2.2 58.7 %conditional.1 = (bf16[512,384]{1,0:T(8,128)(2,1)S(1)}) conditional(s32[]{:T(128)} %convert_element_type.3, (bf16[512,384]{1,0:T(8,128)(2,1)}, bf16[192,384]{1,0:T(8,128)(2,1)}, s32[768]{0:T(1024)S(1)}) %tuple.16, (bf16[512,384]{1,0:T(8,128)(2,1)}, bf16[192,384]{1,0:T(8,128)(2,1)}, s32[768]{0:T(1024)S(1)}) %tuple.17), branch_computations={%region_1.0_spmd, %region_2.0_spmd} | conditional | bytes 8 | solution.py:322
  2.2 58.5 %ladder192.1 = bf16[512,384]{1,0:T(8,128)(2,1)S(1)} custom-call(bf16[512,384]{1,0:T(8,128)(2,1)} %get-tuple-element.31.t_ref, bf16[192,384]{1,0:T(8,128)(2,1)} %get-tuple-element.33.v_ref, s32[768]{0:T(1024)S(1)} %get-tuple-element.22.irreps_ref), custom_call_target="tpu_custom_call" | custom-call | tf_op jit(solution)/shard_map/cond/branch_0_fun/ladder192/pallas_call | solution.py:298
  60.9 0.7 %copy.13 = bf16[512,384]{1,0:T(8,128)(2,1)} copy(bf16[512,384]{1,0:T(8,128)(2,1)S(1)} %get-tuple-element.26) | data formatting | bytes 786432
Async XLA Ops:
  0.0 2.2 %copy-start = (s32[768]{0:T(1024)S(1)}, s32[768]{0:T(1024)}, u32[]{:S(2)}) copy-start(s32[768]{0:T(1024)} %param.7) | copy-start | bytes 9220

commit v4 on v3

--- a/solution.py
+++ b/solution.py
@@ -292,6 +292,280 @@
         copy.wait_send()
 
 
+def narrow(
+    R, t_ref, v_ref, irreps_ref, out_ref,
+    traw, tsend, tmeet, tall, vraw, vpack, vsend, vall, vblock, osend, orecv, ofull,
+    pick, vpick, vrow, unpick,
+    send_sem, recv_sem, local_sem,
+):
+    W, W2, RH = 192, 384, R // 2
+    tight = R == 192
+    YW = 128 if tight else 256
+    split = 48 if tight else 80
+    pair, virt = lax.axis_index("pair"), lax.axis_index("virt")
+    y, zl = pair // 4, pair % 4
+    x, zh, k = virt // 4, (virt // 2) % 2, virt % 2
+
+    def device(x=x, y=y, zh=zh, zl=zl, k=k):
+        return (y * 4 + zl, (x * 2 + zh) * 2 + k)
+
+    xs = [(x + j) % 4 for j in (2, 1, 3)]
+    zs = [(zl + j) % 4 for j in (1, 2, 3)]
+    up, down = (y + 1) % 8, (y + 7) % 8
+    peers = (
+        [device(k=1 - k), device(zh=1 - zh)]
+        + [device(x=o) for o in xs] + [device(zl=o) for o in zs] + [device(y=up), device(y=down)]
+    )
+    barrier = pltpu.get_barrier_semaphore()
+    for peer in peers:
+        pl.semaphore_signal(barrier, inc=1, device_id=peer, device_id_type=MESH)
+
+    mine = pl.multiple_of(k * HALF, HALF)
+    theirs = pl.multiple_of((1 - k) * HALF, HALF)
+    vmine, vtheirs = pl.multiple_of(k * 96, 32), pl.multiple_of((1 - k) * 96, 32)
+    tmine, ttheirs = pl.multiple_of(k * ROWS, ROWS), pl.multiple_of((1 - k) * ROWS, ROWS)
+    other = device(k=1 - k)
+
+    vown = pltpu.make_async_copy(v_ref.at[pl.ds(vmine, 96), :], vraw.at[:, pl.ds(mine, HALF)], local_sem.at[0])
+    vown.start()
+    town = pltpu.make_async_copy(t_ref.at[pl.ds(tmine, ROWS), :], traw.at[:, pl.ds(mine, HALF)], local_sem.at[1])
+    town.start()
+
+    irrep, bins, places = places_of_tiles(irreps_ref)
+    padded = [bins[i] * 256 + places[i] for i in range(TILES)]
+    again = [jnp.where(places[i] == 128, padded[i] + 64, padded[i]) for i in range(TILES)]
+
+    diff = lax.broadcasted_iota(jnp.int32, (TILE, 1024), 1) - lax.broadcasted_iota(jnp.int32, (TILE, 1024), 0)
+    lane = lax.broadcasted_iota(jnp.int32, (1, 1024), 1)
+    lane_irrep = jnp.full((1, 1024), -1, jnp.int32)
+    for i in range(TILES):
+        hit = diff == padded[i] if tight else (diff == padded[i]) | (diff == again[i])
+        vpick[pl.ds(i * TILE, TILE), :] = jnp.where(hit, 1.0, 0.0).astype(BF16)
+        end = (padded[i] if tight else again[i]) + TILE
+        lane_irrep = jnp.where((lane >= padded[i]) & (lane < end), irrep[i], lane_irrep)
+
+    pl.semaphore_wait(barrier, len(peers))
+
+    used = [0]
+    sent = []
+
+    def send(src, dst, to):
+        n = used[0]
+        used[0] += 1
+        copy = pltpu.make_async_remote_copy(
+            src_ref=src, dst_ref=dst, send_sem=send_sem.at[n], recv_sem=recv_sem.at[n],
+            device_id=to, device_id_type=MESH,
+        )
+        copy.start()
+        sent.append(copy)
+        return copy
+
+    vraw_copy = send(v_ref.at[pl.ds(vtheirs, 96), :], vraw.at[:, pl.ds(mine, HALF)], other)
+    traw_copy = send(t_ref.at[pl.ds(ttheirs, ROWS), :], traw.at[:, pl.ds(mine, HALF)], other)
+
+    vown.wait()
+    vraw_copy.wait_recv()
+    packed = jnp.dot(vraw[...], vpick[...], preferred_element_type=F32)
+    for j in range(3):
+        row_irrep = irreps_ref[TILE * (3 * zl + (k * 3 + j) // 2)]
+        part = jnp.where(lane_irrep == row_irrep, packed[j * 32:(j + 1) * 32, :], 0.0)
+        part = sum(part[:, g * YW:(g + 1) * YW] for g in range(1024 // YW))
+        vpack[zl, k, pl.ds(j * 32, 32), :] = part.astype(BF16)
+    mypack = vpack.at[zl, k]
+    zcopies = [send(mypack, mypack, device(zl=o)) for o in zs]
+    dcopies = [send(mypack, mypack, other)]
+
+    for i in range(TILES):
+        pick[pl.ds(i * TILE, TILE), :] = jnp.where(diff == padded[i] + (x % 2) * TILE, 1.0, 0.0).astype(BF16)
+    into = pl.ds(pl.multiple_of(x * 256, 256), 256)
+    tcopies, swaps = [], []
+
+    def scatter(j):
+        rows = pl.ds(*PARTS[j])
+        tsend[rows, :] = jnp.dot(traw[rows, :], pick[...], preferred_element_type=F32).astype(BF16)
+        tcopies.append([
+            send(tsend.at[rows, pl.ds(pl.multiple_of(o * 256, 256), 256)], tmeet.at[rows, into], device(x=o)) for o in xs
+        ])
+        tmeet[rows, into] = tsend[rows, into]
+
+    def swap(j):
+        rows = pl.ds(*PARTS[j])
+        for copy in tcopies[j]:
+            copy.wait_recv()
+        for q in range(2):
+            a, b = tmeet[rows, pl.ds(512 * q, 256)], tmeet[rows, pl.ds(512 * q + 256, 256)]
+            merged = jnp.concatenate([a[:, :128], a[:, 128:] + b[:, :128], b[:, 128:]], axis=1)
+            tall[rows, pl.ds(pl.multiple_of(zh * NVIR + q * W2, 128), W2)] = merged
+        half = tall.at[rows, pl.ds(pl.multiple_of(zh * NVIR, 128), NVIR)]
+        swaps.append(send(half, half, device(zh=1 - zh)))
+
+    town.wait()
+    traw_copy.wait_recv()
+    scatter(0)
+    scatter(1)
+
+    olane = lax.broadcasted_iota(jnp.int32, (1, NVIR), 1)
+    oslot = jnp.zeros((1, NVIR), jnp.int32)
+    opad = jnp.zeros((1, NVIR), jnp.int32)
+    for i in range(TILES):
+        here = (olane >= i * TILE) & (olane < (i + 1) * TILE)
+        oslot = jnp.where(here, bins[i] * W + places[i] + olane - i * TILE, oslot)
+        opad = jnp.where(here, padded[i] + olane - i * TILE, opad)
+    r = lax.broadcasted_iota(jnp.int32, (RH, NVIR), 0)
+    if tight:
+        wants = [k * RH + r]
+    else:
+        wants = [jnp.where(k == 0, r, jnp.where(r < 48, 144 + r, r - 48)), 48 + r]
+    for f, want in enumerate(wants):
+        for m in range(BINS):
+            vrow[f, pl.ds(m * RH, RH), :] = jnp.where(want + m * W == oslot, 1.0, 0.0).astype(BF16)
+
+    for j, o in enumerate(zs):
+        source = (zl + 4 - (1, 2, 3)[j]) % 4
+        zcopies[j].wait_recv()
+        dcopies.append(send(vpack.at[source, k], vpack.at[source, k], other))
+
+    for copy in dcopies:
+        copy.wait_recv()
+    full = jnp.concatenate([vpack[z, c] for z in range(4) for c in range(2)], axis=0)
+    rows_a = jnp.dot(vrow[0], full, preferred_element_type=F32)
+    if tight:
+        folded = rows_a
+    else:
+        rows_b = jnp.dot(vrow[1], full[:, 128:], preferred_element_type=F32)
+        at = lax.broadcasted_iota(jnp.int32, (BINS, RH, 128), 1).reshape(BINS * RH, 128)
+        low = lax.broadcasted_iota(jnp.int32, (BINS * RH, 128), 1) < 64
+        second = (at >= 48 + 144 * (1 - k))
+        folded = jnp.where(second, jnp.where(low, rows_a[:, 128:], rows_b), rows_a[:, :128])
+    vsend[...] = folded.astype(BF16).reshape(BINS, RH, 128)
+
+    first_row = pl.multiple_of(k * RH, 16)
+    myrows = pl.ds(first_row, RH)
+    order = [x, xs[0], xs[1], xs[2]]
+
+    def spot(c):
+        return (c % 2) * 4 + c // 2
+
+    lanes_of = [pl.ds(pl.multiple_of(a * 128, 128), 128) for a in order]
+    xcopies = [send(vsend.at[o], vall.at[spot(y), myrows, lanes_of[0]], device(x=o)) for o in xs]
+    vall[spot(y), myrows, lanes_of[0]] = vsend[x]
+    vcore, ups, downs = [[], [], [], []], [[], [], [], []], [[], [], [], []]
+
+    def share(p, ref):
+        vcore[p].append(send(ref, ref, other))
+
+    def begin(p):
+        piece = vall.at[spot(y), myrows, lanes_of[p]]
+        ups[p].append(send(piece, piece, device(y=up)))
+        downs[p].append(send(piece, piece, device(y=down)))
+        share(p, piece)
+
+    def relay(step, p):
+        from_down, from_up = spot((y + 8 - step) % 8), spot((y + step) % 8)
+        a, b = vall.at[from_down, myrows, lanes_of[p]], vall.at[from_up, myrows, lanes_of[p]]
+        ups[p][-1].wait_recv()
+        if step == 4:
+            downs[p][-1].wait_recv()
+            share(p, a)
+            return
+        if step < 3:
+            ups[p].append(send(a, a, device(y=up)))
+        else:
+            half = vall.at[from_down, pl.ds(first_row, split), lanes_of[p]]
+            ups[p].append(send(half, half, device(y=up)))
+        downs[p][-1].wait_recv()
+        if step < 3:
+            downs[p].append(send(b, b, device(y=down)))
+        else:
+            half = vall.at[from_up, pl.ds(first_row + split, RH - split), lanes_of[p]]
+            downs[p].append(send(half, half, device(y=down)))
+        share(p, a)
+        share(p, b)
+
+    begin(0)
+    swap(0)
+    scatter(2)
+    arrivals = {1: 0, 2: 2, 3: 1}
+    for p in (2, 3, 1):
+        xcopies[arrivals[p]].wait_recv()
+        begin(p)
+    swap(1)
+    scatter(3)
+
+    unpick_at = lax.broadcasted_iota(jnp.int32, (256, NVIR), 0)
+    for m in range(BINS):
+        unpick[pl.ds(m * 256, 256), :] = jnp.where(unpick_at + m * 256 == opad, 1.0, 0.0).astype(BF16)
+
+    def expand(p):
+        for copy in vcore[p]:
+            copy.wait_recv()
+        v = vall[:, :, lanes_of[p]]
+        if tight:
+            left = jnp.concatenate([v[:, :128], jnp.zeros((8, 64, 128), BF16)], axis=1)
+            right = jnp.concatenate([jnp.zeros((8, 128, 128), BF16), v[:, 128:]], axis=1)
+        else:
+            left, fold = v[:, :192], v[:, 192:]
+            turned = pltpu.roll(fold.astype(F32).reshape(8 * 96, 128), 64, 1).astype(BF16).reshape(8, 96, 128)
+            right = jnp.concatenate([fold, turned], axis=1)
+        vblock[p, :, 0:128] = left.reshape(8 * W, 128)
+        vblock[p, :, 128:256] = right.reshape(8 * W, 128)
+
+    ocopies = [[] for _ in BLOCKS]
+
+    def output(p):
+        expand(p)
+        product = jnp.dot(tall[...], vblock[p], preferred_element_type=F32).astype(BF16)
+        if p == 0:
+            orecv[:, into] = product
+            return
+        osend[p - 1] = product
+        for b, block in enumerate(BLOCKS):
+            rows = pl.ds(*block)
+            ocopies[b].append(send(osend.at[p - 1, rows, :], orecv.at[rows, into], device(x=order[p])))
+
+    last, locals_ = [], []
+
+    def finish(b):
+        first, count = BLOCKS[b]
+        rows, to = pl.ds(first, count), pl.ds(tmine + first, count)
+        for copy in ocopies[b]:
+            copy.wait_recv()
+        ofull[rows, :] = jnp.dot(orecv[rows, :], unpick[...], preferred_element_type=F32).astype(BF16)
+        last.append(send(ofull.at[rows, pl.ds(theirs, HALF)], out_ref.at[to, :], other))
+        local = pltpu.make_async_copy(ofull.at[rows, pl.ds(mine, HALF)], out_ref.at[to, :], local_sem.at[2 + b])
+        local.start()
+        locals_.append(local)
+
+    for step in range(1, 4):
+        for p in TURN:
+            relay(step, p)
+        if step < 3:
+            swap(step + 1)
+    for copy in swaps:
+        copy.wait_recv()
+    relay(4, TURN[0])
+    relay(4, TURN[1])
+    output(TURN[0])
+    relay(4, TURN[2])
+    output(TURN[1])
+    relay(4, TURN[3])
+    output(TURN[2])
+    output(TURN[3])
+    finish(0)
+    finish(1)
+    for copy in last:
+        copy.wait_recv()
+    for copy in locals_:
+        copy.wait()
+    for copy in sent:
+        copy.wait_send()
+
+
+PARTS = ((0, 64), (64, 64), (128, 64), (192, 64))
+BLOCKS = ((0, 128), (128, 128))
+TURN = (2, 3, 1, 0)
+
+
 def ladder(width, amplitudes, integrals, irreps):
     vmem = lambda *shape: pltpu.VMEM(shape, BF16)
     W, PW, W2, H = width, width + 64, 2 * width, width // 2
@@ -317,11 +591,37 @@
     )(amplitudes, integrals, irreps)
 
 
+def narrow_ladder(packed_rows, amplitudes, integrals, irreps):
+    vmem = lambda *shape: pltpu.VMEM(shape, BF16)
+    tight = packed_rows == 192
+    half = packed_rows // 2
+    return pl.pallas_call(
+        functools.partial(narrow, packed_rows),
+        out_shape=jax.ShapeDtypeStruct((512, HALF), BF16),
+        in_specs=[
+            pl.BlockSpec(memory_space=pl.ANY), pl.BlockSpec(memory_space=pl.ANY),
+            pl.BlockSpec(memory_space=pltpu.SMEM),
+        ],
+        out_specs=pl.BlockSpec(memory_space=pl.ANY),
+        scratch_shapes=[
+            vmem(ROWS, NVIR), vmem(ROWS, 1024), vmem(ROWS, 1024), vmem(ROWS, 1536),
+            vmem(96, NVIR), vmem(4, 2, 96, 128 if tight else 256), vmem(BINS, half, 128), vmem(8, packed_rows, 512),
+            vmem(4, 1536, 256), vmem(3, ROWS, 256), vmem(ROWS, 1024), vmem(ROWS, NVIR),
+            vmem(NVIR, 1024), vmem(NVIR, 1024), vmem(1 if tight else 2, 4 * half, NVIR), vmem(1024, NVIR),
+            pltpu.SemaphoreType.DMA((SEMS,)), pltpu.SemaphoreType.DMA((SEMS,)), pltpu.SemaphoreType.DMA((4,)),
+        ],
+        compiler_params=pltpu.CompilerParams(
+            collective_id=2 if tight else 3, has_side_effects=True, vmem_limit_bytes=56 << 20
+        ),
+        name="narrow%d" % packed_rows,
+    )(amplitudes, integrals, irreps)
+
+
 def per_device(amplitudes, integrals, irreps):
-    wide = jnp.any(irreps[:-192] == irreps[192:])
-    return lax.cond(
-        wide, functools.partial(ladder, 320), functools.partial(ladder, 192), amplitudes, integrals, irreps
-    )
+    ahead = jnp.pad(irreps, (0, 64), constant_values=-1)
+    over = (irreps[:-128] == irreps[128:]).astype(jnp.int32) + (irreps[:-128] == ahead[192:]).astype(jnp.int32)
+    kernels = [functools.partial(narrow_ladder, 192), functools.partial(narrow_ladder, 288), functools.partial(ladder, 320)]
+    return lax.switch(jnp.max(over), kernels, amplitudes, integrals, irreps)
 
 
 def solution(mesh):

time: 61.9 us -> 60.8 us (0.982)
  Pallas kernels: 58.5 us -> 57 us
    reduce_max x0 -> x1, other arithmetic: none -> 1.54 us  [per_device(): return lax.switch(jnp.max(over), kernels, amplitudes, integrals, irreps)]
    reduce_or x1 -> x0, other arithmetic: 1.5 us -> none  [per_device(): wide = jnp.any(irreps[:-192] == irreps[192:])]
    pallas_call x1, Pallas kernels: 58.5 us -> 57 us  [narrow_ladder(): pl.pallas_call(functools.partial(narrow, packed_rows), out_shape=jax.Shap...]
where the time goes in v4:
time: 60.8 us; the launch traced here: 60.7 us
  Pallas kernels  57 us (94%)
  other arithmetic  1.54 us (3%)
  local copies, waits for them, and re-layouts  0.75 us (1%)
  loops' own time  0.69 us (1%)
  between operations  0.67 us (1%)
    pallas_call x1, Pallas kernels, narrow_ladder(): pl.pallas_call(functools.partial(narrow, packed_rows), out_shape=jax.Shap...  57 us
    reduce_max x1, other arithmetic, per_device(): return lax.switch(jnp.max(over), kernels, amplitudes, integrals, irreps)  1.54 us

profile of v4, /device:TPU:1, one launch (start us, length us, event | category | flops | bytes accessed | tf_op | source)
XLA Modules:
  0.0 60.7 jit_solution(16117054037898276291)
XLA Ops:
  0.0 0.0 copy-start
  0.0 1.5 %add_reduce_fusion = s32[]{:T(128)} fusion(s32[768]{0:T(1024)} %param.8), kind=kLoop, calls=%fused_computation | loop fusion | flops 3839 | bytes 12292 | tf_op jit(solution)/shard_map/reduce_max | solution.py:624
  2.2 0.0 copy-done
  2.2 57.7 %conditional.1 = (bf16[512,384]{1,0:T(8,128)(2,1)S(1)}) conditional(s32[]{:T(128)} %clamp.3, (bf16[512,384]{1,0:T(8,128)(2,1)}, bf16[192,384]{1,0:T(8,128)(2,1)}, s32[768]{0:T(1024)S(1)}) %tuple.21, (bf16[512,384]{1,0:T(8,128)(2,1)}, bf16[192,384]{1,0:T(8,128)(2,1)}, s32[768]{0:T(1024)S(1)}) %tuple.22, (bf16[512,384]{1,0:T(8,128)(2,1)}, ...), branch_computations={%region_1.2_spmd, %region_2.3_spmd, %region_3.4_spmd} | conditional | bytes 8 | solution.py:624
  2.4 57.0 %narrow288.1 = bf16[512,384]{1,0:T(8,128)(2,1)S(1)} custom-call(bf16[512,384]{1,0:T(8,128)(2,1)} %get-tuple-element.30.t_ref, bf16[192,384]{1,0:T(8,128)(2,1)} %get-tuple-element.31.v_ref, s32[768]{0:T(1024)S(1)} %get-tuple-element.32.irreps_ref), custom_call_target="tpu_custom_call" | custom-call | tf_op jit(solution)/shard_map/cond/branch_1_fun/narrow288/pallas_call | solution.py:598
  59.9 0.7 %copy.11 = bf16[512,384]{1,0:T(8,128)(2,1)} copy(bf16[512,384]{1,0:T(8,128)(2,1)S(1)} %get-tuple-element.36) | data formatting | bytes 786432
Async XLA Ops:
  0.0 2.2 %copy-start = (s32[768]{0:T(1024)S(1)}, s32[768]{0:T(1024)}, u32[]{:S(2)}) copy-start(s32[768]{0:T(1024)} %param.8) | copy-start | bytes 9220

commit v5 on v4

--- a/solution.py
+++ b/solution.py
@@ -449,16 +449,16 @@
     lanes_of = [pl.ds(pl.multiple_of(a * 128, 128), 128) for a in order]
     xcopies = [send(vsend.at[o], vall.at[spot(y), myrows, lanes_of[0]], device(x=o)) for o in xs]
     vall[spot(y), myrows, lanes_of[0]] = vsend[x]
-    vcore, ups, downs = [[], [], [], []], [[], [], [], []], [[], [], [], []]
-
-    def share(p, ref):
-        vcore[p].append(send(ref, ref, other))
+    whole, vcore, ups, downs = [], [[], [], [], []], [[], [], [], []], [[], [], [], []]
+
+    def share(c):
+        block = vall.at[spot(c), myrows]
+        whole.append(send(block, block, other))
 
     def begin(p):
         piece = vall.at[spot(y), myrows, lanes_of[p]]
         ups[p].append(send(piece, piece, device(y=up)))
         downs[p].append(send(piece, piece, device(y=down)))
-        share(p, piece)
 
     def relay(step, p):
         from_down, from_up = spot((y + 8 - step) % 8), spot((y + step) % 8)
@@ -466,7 +466,7 @@
         ups[p][-1].wait_recv()
         if step == 4:
             downs[p][-1].wait_recv()
-            share(p, a)
+            vcore[p].append(send(a, a, other))
             return
         if step < 3:
             ups[p].append(send(a, a, device(y=up)))
@@ -479,8 +479,6 @@
         else:
             half = vall.at[from_up, pl.ds(first_row + split, RH - split), lanes_of[p]]
             downs[p].append(send(half, half, device(y=down)))
-        share(p, a)
-        share(p, b)
 
     begin(0)
     swap(0)
@@ -489,14 +487,18 @@
     for p in (2, 3, 1):
         xcopies[arrivals[p]].wait_recv()
         begin(p)
+    share(y)
     swap(1)
     scatter(3)
+    swap(2)
 
     unpick_at = lax.broadcasted_iota(jnp.int32, (256, NVIR), 0)
     for m in range(BINS):
         unpick[pl.ds(m * 256, 256), :] = jnp.where(unpick_at + m * 256 == opad, 1.0, 0.0).astype(BF16)
 
     def expand(p):
+        while whole:
+            whole.pop(0).wait_recv()
         for copy in vcore[p]:
             copy.wait_recv()
         v = vall[:, :, lanes_of[p]]
@@ -539,12 +541,14 @@
     for step in range(1, 4):
         for p in TURN:
             relay(step, p)
-        if step < 3:
-            swap(step + 1)
+        share((y + 8 - step) % 8)
+        share((y + step) % 8)
+        if step == 1:
+            swap(3)
+    relay(4, TURN[0])
+    relay(4, TURN[1])
     for copy in swaps:
         copy.wait_recv()
-    relay(4, TURN[0])
-    relay(4, TURN[1])
     output(TURN[0])
     relay(4, TURN[2])
     output(TURN[1])

time: 60.8 us -> 60.3 us (level)
  no operation moved by 1% of the time
where the time goes in v5:
time: 60.3 us; the launch traced here: 60.2 us
  Pallas kernels  56.5 us (94%)
  other arithmetic  1.54 us (3%)
  local copies, waits for them, and re-layouts  0.75 us (1%)
  loops' own time  0.69 us (1%)
  between operations  0.67 us (1%)
    pallas_call x1, Pallas kernels, narrow_ladder(): pl.pallas_call(functools.partial(narrow, packed_rows), out_shape=jax.Shap...  56.5 us
    reduce_max x1, other arithmetic, per_device(): return lax.switch(jnp.max(over), kernels, amplitudes, integrals, irreps)  1.54 us

profile of v5, /device:TPU:1, one launch (start us, length us, event | category | flops | bytes accessed | tf_op | source)
XLA Modules:
  0.0 60.2 jit_solution(652395909777670304)
XLA Ops:
  0.0 0.0 copy-start
  0.0 1.5 %add_reduce_fusion = s32[]{:T(128)} fusion(s32[768]{0:T(1024)} %param.8), kind=kLoop, calls=%fused_computation | loop fusion | flops 3839 | bytes 12292 | tf_op jit(solution)/shard_map/reduce_max | solution.py:628
  2.2 0.0 copy-done
  2.2 57.2 %conditional.1 = (bf16[512,384]{1,0:T(8,128)(2,1)S(1)}) conditional(s32[]{:T(128)} %clamp.3, (bf16[512,384]{1,0:T(8,128)(2,1)}, bf16[192,384]{1,0:T(8,128)(2,1)}, s32[768]{0:T(1024)S(1)}) %tuple.21, (bf16[512,384]{1,0:T(8,128)(2,1)}, bf16[192,384]{1,0:T(8,128)(2,1)}, s32[768]{0:T(1024)S(1)}) %tuple.22, (bf16[512,384]{1,0:T(8,128)(2,1)}, ...), branch_computations={%region_1.2_spmd, %region_2.3_spmd, %region_3.4_spmd} | conditional | bytes 8 | solution.py:628
  2.4 56.5 %narrow288.1 = bf16[512,384]{1,0:T(8,128)(2,1)S(1)} custom-call(bf16[512,384]{1,0:T(8,128)(2,1)} %get-tuple-element.30.t_ref, bf16[192,384]{1,0:T(8,128)(2,1)} %get-tuple-element.31.v_ref, s32[768]{0:T(1024)S(1)} %get-tuple-element.32.irreps_ref), custom_call_target="tpu_custom_call" | custom-call | tf_op jit(solution)/shard_map/cond/branch_1_fun/narrow288/pallas_call | solution.py:602
  59.4 0.7 %copy.11 = bf16[512,384]{1,0:T(8,128)(2,1)} copy(bf16[512,384]{1,0:T(8,128)(2,1)S(1)} %get-tuple-element.36) | data formatting | bytes 786432
Async XLA Ops:
  0.0 2.2 %copy-start = (s32[768]{0:T(1024)S(1)}, s32[768]{0:T(1024)}, u32[]{:S(2)}) copy-start(s32[768]{0:T(1024)} %param.8) | copy-start | bytes 9220
